TPU v7x, 1024 devices: a whole 4x4x32 slice. The times are simulated.
1024 devices in a mesh: dp: 32 (over z_lo, y), owner: 32 (over x, z_hi, core).
Axes of the slice: x: 4, y: 4, z: 32 (z_hi: 4, z_lo: 8; z = z_hi * 8 + z_lo), core: 2. Of those that a mesh axis runs over, the one named last changes fastest.
Arguments:
- activations: bfloat16 [65536, 512], P('dp'), may hold values from -6 to 6
- cotangent: bfloat16 [32, 512, 65536], P(None, 'owner', 'dp'), may hold values from -0.046875 to 0.046875
- left_basis: float32 [32, 512, 512], P('dp'), may hold values from -1 to 1, as said below
- right_basis: float32 [32, 512, 512], P('dp'), may hold values from -1 to 1, as said below
- first_moment: float32 [32, 512, 512], P('dp', None, 'owner'), may hold values from -4 to 4
- second_moment: float32 [32, 512, 512], P('dp', None, 'owner'), may hold values from 0.01 to 1
- master_weight: float32 [32, 512, 512], P('dp', 'owner'), may hold values from -0.3125 to 0.3125
Outputs:
- new_weight: float32 [32, 512, 512], P('dp', 'owner')
- compute_weight: bfloat16 [32, 512, 512], P('dp', 'owner')
- new_first: float32 [32, 512, 512], P('dp', None, 'owner')
- new_second: float32 [32, 512, 512], P('dp', None, 'owner')
Inputs may be any that keep to these rules, and one draw needn't show every extreme that they name: Each block of left_basis is an orthogonal matrix. Each block of right_basis is an orthogonal matrix.
All inputs are finite; a program needn't handle non-finite values.
Results may differ from a plain program's by a relative error of at most 0.0013.
Values sent between devices are 32-bit elements; how exact they have to be, the bound alone decides.
No kernel may reach another device: no remote copies, remote signals or barrier semaphores. Data moves between devices by JAX's collectives and lax.ppermute only.
A program may use at most 32 MiB of HBM per device.

v0:
```python
import jax
import jax.numpy as jnp
from jax import lax
from jax.sharding import PartitionSpec as P

beta_one = 0.9
beta_two = 0.95
correct_one = 1.0 - 0.9**10
correct_two = 1.0 - 0.95**10
epsilon = 1e-08
learning_rate = 0.01


def shards(
    activations, cotangent, left_basis, right_basis, first_moment, second_moment, master_weight
):
    highest = lax.Precision.HIGHEST
    gradient_rows = lax.psum_scatter(
        jnp.einsum("bwt,tr->bwr", cotangent, activations, preferred_element_type=jnp.float32),
        "dp",
        scatter_dimension=0,
        tiled=True,
    )[0]
    left_matrix = left_basis[0]
    right_matrix = right_basis[0]
    strip_rows = gradient_rows.shape[0]
    owner_index = lax.axis_index("owner")
    right_columns = lax.dynamic_slice_in_dim(right_matrix, owner_index * strip_rows, strip_rows, 1)
    turned = jnp.dot(
        lax.all_gather(gradient_rows, "owner", axis=0, tiled=True), right_columns, precision=highest
    )
    rotated = jnp.einsum("ij,ik->jk", left_matrix, turned, precision=highest)
    first_new = beta_one * first_moment[0] + (1.0 - beta_one) * rotated
    second_new = beta_two * second_moment[0] + (1.0 - beta_two) * rotated * rotated
    direction = first_new / correct_one / (jnp.sqrt(second_new / correct_two) + epsilon)
    left_rows = lax.dynamic_slice_in_dim(left_matrix, owner_index * strip_rows, strip_rows, 0)
    partial_value = jnp.dot(
        left_rows, lax.all_gather(direction, "owner", axis=1, tiled=True), precision=highest
    )
    update = jnp.einsum("ik,jk->ij", partial_value, right_matrix, precision=highest)
    weight_new = master_weight[0] - learning_rate * update
    rounded_weight = weight_new.astype(jnp.bfloat16)
    return (weight_new[None], rounded_weight[None], first_new[None], second_new[None])


def solution(mesh):
    in_specs = (
        P("dp", None),
        P(None, "owner", "dp"),
        P("dp", None, None),
        P("dp", None, None),
        P("dp", None, "owner"),
        P("dp", None, "owner"),
        P("dp", "owner", None),
    )
    out_specs = (
        P("dp", "owner", None),
        P("dp", "owner", None),
        P("dp", None, "owner"),
        P("dp", None, "owner"),
    )
    return jax.shard_map(shards, mesh=mesh, in_specs=in_specs, out_specs=out_specs, check_vma=False)
```

profile of v0, /device:TPU:1, one launch (start us, length us, event | category | flops | bytes accessed | tf_op | source)
XLA Modules:
  0.0 502.9 jit_solution(15986335363729275551)
XLA Ops:
  7.2 0.0 copy-start
  7.2 0.0 copy-start.1
  7.2 0.0 reduce-scatter.2.cloned.1.call-start
  7.2 1.5 copy-done
  8.8 3.8 fusion
  12.6 0.0 copy-start.4
  12.6 0.0 copy-start.5
  12.6 0.0 reduce-scatter.2.cloned.1.call-update
  12.6 0.0 all-gather.6.cloned.1.call-start
  12.7 234.7 %reduce-scatter.2.cloned.1.call-done = f32[1,16,512]{2,1,0:T(8,128)} async-done(((f32[32,16,512]{2,1,0:T(8,128)}), f32[1,16,512]{2,1,0:T(8,128)}) %reduce-scatter.2.cloned.1.call-update) | async-done | bytes 32784 | tf_op jit(solution)/shard_map/reduce_scatter | solution.py:18
  247.4 0.0 all-gather.6.cloned.1.call-update
  247.4 0.0 all-gather.4.cloned.1.call-start
  247.4 0.0 copy-start.6
  247.5 135.0 %all-gather.6.cloned.1.call-done = f32[1,512,512]{2,1,0:T(8,128)} async-done(((f32[1,16,512]{2,1,0:T(8,128)}), f32[1,512,512]{2,1,0:T(8,128)}) %all-gather.6.cloned.1.call-update) | async-done | bytes 1048592 | tf_op jit(solution)/shard_map/all_gather | solution.py:30
  382.4 0.0 copy-done.1
  382.4 0.0 copy-start.2
  382.4 2.4 fusion.5
  384.8 0.0 copy-done.4
  384.8 0.0 copy-done.5
  384.8 0.0 copy-done.2
  384.8 1.3 fusion.14
  386.1 0.0 all-gather.4.cloned.1.call-update
  386.2 106.4 %all-gather.4.cloned.1.call-done = f32[512,512]{0,1:T(8,128)} async-done(((f32[512,16]{0,1:T(8,128)}), f32[512,512]{0,1:T(8,128)}) %all-gather.4.cloned.1.call-update) | async-done | bytes 1048592 | tf_op jit(solution)/shard_map/all_gather | solution.py:38
  492.5 2.2 fusion.10
  494.7 0.0 copy-done.6
  494.7 1.0 fusion.2
  495.7 0.0 copy-start.3
  495.7 0.6 convert_bitcast_fusion
  496.3 0.0 copy-done.3
Async XLA Ops:
  7.2 1.6 copy-start
  7.2 375.2 %copy-start.1 = (f32[1,512,512]{2,1,0:T(8,128)S(1)}, f32[1,512,512]{2,1,0:T(8,128)}, u32[]{:S(2)}) copy-start(f32[1,512,512]{2,1,0:T(8,128)} %param.10) | copy-start | bytes 3145732
  7.2 240.2 %reduce-scatter.2.cloned.1.call-start = ((), (), s32[]{:S(2)}) async-start(), calls=%async_computation.1 | async-start | bytes 1081344 | tf_op jit(solution)/shard_map/reduce_scatter | solution.py:18
  12.6 372.2 %copy-start.4 = (f32[1,512,16]{1,2,0:T(8,128)S(1)}, f32[1,512,16]{1,2,0:T(8,128)}, u32[]{:S(2)}) copy-start(f32[1,512,16]{1,2,0:T(8,128)} %param.12) | copy-start | bytes 98308
  12.6 372.2 %copy-start.5 = (f32[1,512,16]{1,2,0:T(8,128)S(1)}, f32[1,512,16]{1,2,0:T(8,128)}, u32[]{:S(2)}) copy-start(f32[1,512,16]{1,2,0:T(8,128)} %param.11) | copy-start | bytes 98308
  12.6 369.8 %all-gather.6.cloned.1.call-start = ((), (), s32[]{:S(2)}) async-start(), calls=%async_computation.3 | async-start | bytes 1081344 | tf_op jit(solution)/shard_map/all_gather | solution.py:30
  247.4 245.1 %all-gather.4.cloned.1.call-start = ((), (), s32[]{:S(2)}) async-start(), calls=%async_computation.2 | async-start | bytes 1081344 | tf_op jit(solution)/shard_map/all_gather | solution.py:38
  247.4 247.3 %copy-start.6 = (f32[1,16,512]{2,1,0:T(8,128)S(1)}, f32[1,16,512]{2,1,0:T(8,128)}, u32[]{:S(2)}) copy-start(f32[1,16,512]{2,1,0:T(8,128)} %param.13) | copy-start | bytes 98308
  382.4 2.4 copy-start.2
  495.7 0.6 copy-start.3
Sparse Core Ops, SparseCore 0:
  12.7 234.5 reduce-scatter.1
  252.4 129.9 all-gather.5
  388.1 104.4 all-gather.3
where the time goes:
time: 503 us
  waiting for transfers between devices  476 us (95%)
  between operations  13.8 us (3%)
  matrix products  10.7 us (2%)
    reduce_scatter x1, waiting for transfers between devices, shards(): lax.psum_scatter(jnp.einsum('bwt,tr->bwr', cotangent, activations, prefer...  235 us
    all_gather x1, waiting for transfers between devices, shards(): lax.all_gather(gradient_rows, 'owner', axis=0, tiled=True)  135 us
    all_gather x1, waiting for transfers between devices, shards(): lax.all_gather(direction, 'owner', axis=1, tiled=True)  106 us
  transfers between devices with their start and end apart: 3, of which 3 were waited for; matrix products, arithmetic and copies ran while one was open for 0% of the time, Pallas kernels for 0%

commit v1 on v0

v1 whole, which is shorter than its diff:
```python
import jax
import jax.numpy as jnp
from jax import lax
from jax.sharding import PartitionSpec as P

beta_one = 0.9
beta_two = 0.95
correct_one = 1.0 - 0.9**10
correct_two = 1.0 - 0.95**10
epsilon = 1e-08
learning_rate = 0.01

near_groups = [[(2 * q + p) * 4 + y for p in range(2) for y in range(4)] for q in range(4)]
quad_groups = [[(2 * q + p) * 4 + y for q in range(4)] for p in range(2) for y in range(4)]


def swap_strips(value):
    rows, columns = value.shape
    owners = columns // rows
    packed = value.reshape(rows, owners, rows).transpose(1, 0, 2).reshape(owners, 2, rows * rows // 2)
    packed = lax.all_to_all(packed, "owner", 0, 0, tiled=True)
    return packed.reshape(owners, rows, rows).transpose(2, 0, 1).reshape(rows, columns)


def shards(
    activations, cotangent, left_basis, right_basis, first_moment, second_moment, master_weight
):
    precision = lax.Precision.HIGH
    left_matrix = left_basis[0]
    right_matrix = right_basis[0]
    partial = jnp.einsum("bwt,tr->bwr", cotangent, activations, preferred_element_type=jnp.float32)
    partial = partial.reshape(4, 8, 16, 512)
    near = lax.all_to_all(partial, "dp", 1, 1, axis_index_groups=near_groups, tiled=True).sum(1)
    far = lax.all_to_all(near, "dp", 0, 0, axis_index_groups=quad_groups, tiled=True)
    gradient_rows = far.sum(0)
    turned = swap_strips(jnp.dot(gradient_rows, right_matrix, precision=precision))
    rotated = jnp.dot(turned, left_matrix, precision=precision)
    first_new = beta_one * first_moment[0].T + (1.0 - beta_one) * rotated
    second_new = beta_two * second_moment[0].T + (1.0 - beta_two) * rotated * rotated
    direction = first_new / correct_one / (jnp.sqrt(second_new / correct_two) + epsilon)
    half = swap_strips(jnp.einsum("cj,ij->ci", direction, left_matrix, precision=precision))
    update = jnp.einsum("ik,jk->ij", half, right_matrix, precision=precision)
    weight_new = master_weight[0] - learning_rate * update
    rounded_weight = weight_new.astype(jnp.bfloat16)
    return (weight_new[None], rounded_weight[None], first_new.T[None], second_new.T[None])


def solution(mesh):
    in_specs = (
        P("dp", None),
        P(None, "owner", "dp"),
        P("dp", None, None),
        P("dp", None, None),
        P("dp", None, "owner"),
        P("dp", None, "owner"),
        P("dp", "owner", None),
    )
    out_specs = (
        P("dp", "owner", None),
        P("dp", "owner", None),
        P("dp", None, "owner"),
        P("dp", None, "owner"),
    )
    return jax.shard_map(shards, mesh=mesh, in_specs=in_specs, out_specs=out_specs, check_vma=False)
```

time: 503 us -> 136 us (0.27)
  waiting for transfers between devices: 476 us -> 29.6 us
  blocking collectives: 0 us -> 68.7 us
  starting transfers between devices: 0.12 us -> 18.8 us
  between operations: 13.8 us -> 0.78 us
    all_gather x2 -> x0, waiting for transfers between devices: 241 us -> none  [the longest x1 135 us: shards(): lax.all_gather(gradient_rows, 'owner', axis=0, tiled=True)]
    reduce_scatter x1 -> x0, waiting for transfers between devices: 235 us -> none  [shards(): lax.psum_scatter(jnp.einsum('bwt,tr->bwr', cotangent, activations, prefer...]
    all_to_all x0 -> x2, blocking collectives: none -> 68.7 us  [the longest x1 52.3 us: swap_strips(): packed = lax.all_to_all(packed, 'owner', 0, 0, tiled=True)]
    all_to_all x0 -> x2, waiting for transfers between devices: none -> 29.6 us  [the longest x1 23.5 us: swap_strips(): packed = lax.all_to_all(packed, 'owner', 0, 0, tiled=True)]
    all_to_all x0 -> x2, starting transfers between devices: none -> 18.8 us  [the longest x1 14.9 us: shards(): lax.all_to_all(near, 'dp', 0, 0, axis_index_groups=quad_groups, tiled=True)]
  transfers between devices with their start and end apart: 3 -> 2, of which waited for: 3 -> 2; matrix products, arithmetic and copies ran while one was open for 0% -> 2% of each run, Pallas kernels for 0% -> 0%
where the time goes in v1:
time: 136 us; the launch traced here: 135 us
  blocking collectives  68.7 us (51%)
  waiting for transfers between devices  29.6 us (22%)
  starting transfers between devices  18.8 us (14%)
  matrix products  9.32 us (7%)
  local copies, waits for them, and re-layouts  5.98 us (4%)
  other arithmetic  1.98 us (1%)
    all_to_all x1, blocking collectives, swap_strips(): packed = lax.all_to_all(packed, 'owner', 0, 0, tiled=True)  52.3 us
    all_to_all x1, waiting for transfers between devices, swap_strips(): packed = lax.all_to_all(packed, 'owner', 0, 0, tiled=True)  23.5 us
    all_to_all x1, blocking collectives, shards(): lax.all_to_all(partial, 'dp', 1, 1, axis_index_groups=near_groups, tiled=...  16.5 us
    all_to_all x1, starting transfers between devices, shards(): lax.all_to_all(near, 'dp', 0, 0, axis_index_groups=quad_groups, tiled=True)  14.9 us
    all_to_all x1, waiting for transfers between devices, shards(): lax.all_to_all(near, 'dp', 0, 0, axis_index_groups=quad_groups, tiled=True)  6.05 us
    unnamed x13, local copies, waits for them, and re-layouts  4.24 us
    all_to_all x1, starting transfers between devices, swap_strips(): packed = lax.all_to_all(packed, 'owner', 0, 0, tiled=True)  3.9 us
    dot_general x1, matrix products, shards(): jnp.einsum('bwt,tr->bwr', cotangent, activations, preferred_element_type=...  2.83 us
  transfers between devices with their start and end apart: 2, of which 2 were waited for; matrix products, arithmetic and copies ran while one was open for 2% of the time, Pallas kernels for 0%

profile of v1, /device:TPU:1, one launch (start us, length us, event | category | flops | bytes accessed | tf_op | source)
XLA Modules:
  0.0 135.1 jit_solution(7157584904604076227)
XLA Ops:
  0.6 0.0 copy-start
  0.6 1.6 %copy-done = bf16[32,16,2048]{2,1,0:T(8,128)(2,1)S(1)} copy-done((bf16[32,16,2048]{2,1,0:T(8,128)(2,1)S(1)}, bf16[32,16,2048]{2,1,0:T(8,128)(2,1)}, u32[]{:S(2)}) %copy-start) | copy-done | bytes 2097176
  2.2 2.8 %fusion = f32[32,16,512]{2,1,0:T(8,128)S(1)} fusion(bf16[32,16,2048]{2,1,0:T(8,128)(2,1)S(1)} %copy-done, bf16[2048,512]{1,0:T(8,128)(2,1)} %param.7), kind=kOutput, calls=%fused_computation | convolution fusion | flops 1073741824 | bytes 5242880 | tf_op jit(solution)/shard_map/bwt,tr->bwr/dot_general | solution.py:31
  5.1 0.1 copy.37
  5.1 16.5 %all_to_all.20 = f32[4,8,16,512]{3,2,0,1:T(8,128)S(1)} all-to-all(f32[4,8,16,512]{3,2,0,1:T(8,128)S(1)} %copy.37), channel_id=1, replica_groups={{0,32,64,96,128,160,192,224},{256,288,320,352,384,416,448,480},{512,544..., dimensions={1} | all-to-all | bytes 2097152 | tf_op jit(solution)/shard_map/all_to_all | solution.py:33
  21.6 0.7 reduce_sum.18
  22.3 14.9 %all-to-all-start.1 = ((f32[4,16,512]{2,1,0:T(8,128)}), f32[4,16,512]{2,1,0:T(8,128)S(1)}, u32[]{:S(2)}, u32[]{:S(2)}) async-start(f32[4,16,512]{2,1,0:T(8,128)} %reduce_sum.18), calls=%async_computation.1 | async-start | bytes 262144 | tf_op jit(solution)/shard_map/all_to_all | solution.py:34
  37.2 0.0 copy-start.1
  37.2 2.6 %copy.38 = f32[1,512,512]{1,2,0:T(8,128)} copy(f32[1,512,512]{2,1,0:T(8,128)} %param.10) | data formatting | bytes 2097152 | tf_op args[3]
  39.8 6.1 %all-to-all-done.1 = f32[4,16,512]{2,1,0:T(8,128)S(1)} async-done(((f32[4,16,512]{2,1,0:T(8,128)}), f32[4,16,512]{2,1,0:T(8,128)S(1)}, u32[]{:S(2)}, u32[]{:S(2)}) %all-to-all-start.1) | async-done | bytes 131104 | tf_op jit(solution)/shard_map/all_to_all | solution.py:34
  45.9 2.6 %convolution_bitcast_fusion.1 = f32[32,16,16]{0,1,2:T(8,128)S(1)} fusion(f32[32,16,512]{2,1,0:T(8,128)} %bitcast.72, f32[16,512]{1,0:T(8,128)S(1)} %reduce_sum.19), kind=kOutput, calls=%fused_computation.3 | convolution fusion | flops 25165824 | bytes 1114112 | tf_op jit(solution)/shard_map/dot_general | solution.py:36
  48.5 0.1 copy.40
  48.6 0.1 copy.41
  48.7 52.3 %all_to_all.21 = f32[32,2,128]{2,1,0:T(2,128)S(1)} all-to-all(f32[32,2,128]{2,1,0:T(2,128)S(1)} %copy.41), channel_id=1, replica_groups=mesh['dp'=32,'owner'=32] {'owner'}, dimensions={0} | all-to-all | bytes 65536 | tf_op jit(solution)/shard_map/all_to_all | solution.py:21
  100.9 0.1 copy.42
  101.0 0.1 copy.43
  101.2 0.2 reshape.45
  101.3 0.0 copy-done.1
  101.4 0.0 copy-start.3
  101.4 0.0 copy-start.4
  101.4 0.4 fusion.4
  101.7 2.2 %convolution_bitcast_fusion = f32[32,16,16]{0,1,2:T(8,128)S(1)} fusion(f32[32,16,512]{2,1,0:T(8,128)S(1)} %bitcast.71, f32[16,512]{1,0:T(8,128)S(1)} %fusion.4, f32[1,512,16]{1,2,0:T(8,128)} %param.12, f32[1,512,16]{1,2,0:T(8,128)} %param.11), kind=kOutput, calls=%fused_computation.2 | convolution fusion | flops 25255936 | bytes 1179648 | tf_op jit(solution)/shard_map/cj,ij->ci/dot_general | solution.py:41
  104.0 0.0 copy-start.2
  104.0 0.7 copy.46
  104.7 3.9 %all-to-all-start.3 = ((f32[32,2,128]{2,1,0:T(2,128)}), f32[32,2,128]{2,1,0:T(2,128)S(1)}, u32[]{:S(2)}, u32[]{:S(2)}) async-start(f32[32,2,128]{2,1,0:T(2,128)} %copy.46), calls=%async_computation.3 | async-start | bytes 65536 | tf_op jit(solution)/shard_map/all_to_all | solution.py:21
  108.6 0.0 copy-done.3
  108.6 0.0 copy-done.4
  108.7 0.6 fusion.16
  109.3 23.5 %all-to-all-done.3 = f32[32,2,128]{2,1,0:T(2,128)S(1)} async-done(((f32[32,2,128]{2,1,0:T(2,128)}), f32[32,2,128]{2,1,0:T(2,128)S(1)}, u32[]{:S(2)}, u32[]{:S(2)}) %all-to-all-start.3) | async-done | bytes 32800 | tf_op jit(solution)/shard_map/all_to_all | solution.py:21
  132.8 0.1 copy.47
  132.9 0.1 copy.48
  133.1 0.2 reshape.48
  133.2 0.0 copy-done.2
  133.2 1.3 fusion.2
  134.5 0.0 copy-start.5
  134.5 0.6 convert_bitcast_fusion
  135.1 0.0 copy-done.5
  (2 shorter events, 0.1 us)
Async XLA Ops:
  0.6 1.6 %copy-start = (bf16[32,16,2048]{2,1,0:T(8,128)(2,1)S(1)}, bf16[32,16,2048]{2,1,0:T(8,128)(2,1)}, u32[]{:S(2)}) copy-start(bf16[32,16,2048]{2,1,0:T(8,128)(2,1)} %param.8) | copy-start | bytes 6291460
  22.3 23.6 %all-to-all-start.1 = ((f32[4,16,512]{2,1,0:T(8,128)}), f32[4,16,512]{2,1,0:T(8,128)S(1)}, u32[]{:S(2)}, u32[]{:S(2)}) async-start(f32[4,16,512]{2,1,0:T(8,128)} %reduce_sum.18), calls=%async_computation.1 | async-start | bytes 262144 | tf_op jit(solution)/shard_map/all_to_all | solution.py:34
  37.2 64.1 %copy-start.1 = (f32[1,512,512]{2,1,0:T(8,128)S(1)}, f32[1,512,512]{2,1,0:T(8,128)}, u32[]{:S(2)}) copy-start(f32[1,512,512]{2,1,0:T(8,128)} %param.9) | copy-start | bytes 3145732
  101.4 7.3 %copy-start.3 = (f32[1,512,16]{1,2,0:T(8,128)S(1)}, f32[1,512,16]{1,2,0:T(8,128)}, u32[]{:S(2)}) copy-start(f32[1,512,16]{1,2,0:T(8,128)} %param.12) | copy-start | bytes 98308
  101.4 7.3 %copy-start.4 = (f32[1,512,16]{1,2,0:T(8,128)S(1)}, f32[1,512,16]{1,2,0:T(8,128)}, u32[]{:S(2)}) copy-start(f32[1,512,16]{1,2,0:T(8,128)} %param.11) | copy-start | bytes 98308
  104.0 29.3 %copy-start.2 = (f32[1,512,512]{2,1,0:T(8,128)S(1)}, f32[1,512,512]{2,1,0:T(8,128)}, u32[]{:S(2)}) copy-start(f32[1,512,512]{2,1,0:T(8,128)} %param.10) | copy-start | bytes 3145732
  104.7 28.1 %all-to-all-start.3 = ((f32[32,2,128]{2,1,0:T(2,128)}), f32[32,2,128]{2,1,0:T(2,128)S(1)}, u32[]{:S(2)}, u32[]{:S(2)}) async-start(f32[32,2,128]{2,1,0:T(2,128)} %copy.46), calls=%async_computation.3 | async-start | bytes 65536 | tf_op jit(solution)/shard_map/all_to_all | solution.py:21
  134.5 0.6 copy-start.5

commit v2 on v1

--- a/solution.py
+++ b/solution.py
@@ -11,14 +11,18 @@
 learning_rate = 0.01
 
 near_groups = [[(2 * q + p) * 4 + y for p in range(2) for y in range(4)] for q in range(4)]
-quad_groups = [[(2 * q + p) * 4 + y for q in range(4)] for p in range(2) for y in range(4)]
+quad_groups = [[(2 * q + p) * 4 + y for q in (2, 3, 0, 1)] for p in range(2) for y in range(4)]
+
+owner_order = [(x * 4 + h) * 2 + c for x in range(4) for h in (2, 3, 0, 1) for c in range(2)]
 
 
 def swap_strips(value):
     rows, columns = value.shape
     owners = columns // rows
     packed = value.reshape(rows, owners, rows).transpose(1, 0, 2).reshape(owners, 2, rows * rows // 2)
-    packed = lax.all_to_all(packed, "owner", 0, 0, tiled=True)
+    packed = jnp.roll(packed.reshape(4, 4, -1, 128), 2, 1).reshape(owners, 2, 128)
+    packed = lax.all_to_all(packed, "owner", 0, 0, axis_index_groups=[owner_order], tiled=True)
+    packed = jnp.roll(packed.reshape(4, 4, -1, 128), 2, 1)
     return packed.reshape(owners, rows, rows).transpose(2, 0, 1).reshape(rows, columns)
 
 
@@ -31,6 +35,7 @@
     partial = jnp.einsum("bwt,tr->bwr", cotangent, activations, preferred_element_type=jnp.float32)
     partial = partial.reshape(4, 8, 16, 512)
     near = lax.all_to_all(partial, "dp", 1, 1, axis_index_groups=near_groups, tiled=True).sum(1)
+    near = jnp.roll(near, 2, 0)
     far = lax.all_to_all(near, "dp", 0, 0, axis_index_groups=quad_groups, tiled=True)
     gradient_rows = far.sum(0)
     turned = swap_strips(jnp.dot(gradient_rows, right_matrix, precision=precision))

time: 136 us -> 118 us (0.87)
  waiting for transfers between devices: 29.6 us -> 4.31 us
  starting transfers between devices: 18.8 us -> 38.5 us
  blocking collectives: 68.7 us -> 55.2 us
  other arithmetic: 1.98 us -> 3.45 us
    all_to_all x1, waiting for transfers between devices: 23.5 us -> 3.33 us  [swap_strips(): lax.all_to_all(packed, 'owner', 0, 0, axis_index_groups=[owner_order], ti...]
    all_to_all x1, starting transfers between devices: 3.9 us -> 23.4 us  [swap_strips(): lax.all_to_all(packed, 'owner', 0, 0, axis_index_groups=[owner_order], ti...]
    all_to_all x1, blocking collectives: 52.3 us -> 38.7 us  [swap_strips(): lax.all_to_all(packed, 'owner', 0, 0, axis_index_groups=[owner_order], ti...]
    all_to_all x1, waiting for transfers between devices: 6.05 us -> 0.97 us  [shards(): lax.all_to_all(near, 'dp', 0, 0, axis_index_groups=quad_groups, tiled=True)]
    unnamed x13 -> x11, local copies, waits for them, and re-layouts: 4.24 us -> 4.85 us
  transfers between devices with their start and end apart: 2 -> 2, of which waited for: 2 -> 2; matrix products, arithmetic and copies ran while one was open for 2% -> 3% of each run, Pallas kernels for 0% -> 0%
where the time goes in v2:
time: 118 us
  blocking collectives  55.2 us (47%)
  starting transfers between devices  38.5 us (33%)
  matrix products  9.37 us (8%)
  local copies, waits for them, and re-layouts  5.86 us (5%)
  waiting for transfers between devices  4.31 us (4%)
  other arithmetic  3.45 us (3%)
    all_to_all x1, blocking collectives, swap_strips(): lax.all_to_all(packed, 'owner', 0, 0, axis_index_groups=[owner_order], ti...  38.7 us
    all_to_all x1, starting transfers between devices, swap_strips(): lax.all_to_all(packed, 'owner', 0, 0, axis_index_groups=[owner_order], ti...  23.4 us
    all_to_all x1, blocking collectives, shards(): lax.all_to_all(partial, 'dp', 1, 1, axis_index_groups=near_groups, tiled=...  16.5 us
    all_to_all x1, starting transfers between devices, shards(): lax.all_to_all(near, 'dp', 0, 0, axis_index_groups=quad_groups, tiled=True)  15.2 us
    unnamed x11, local copies, waits for them, and re-layouts  4.85 us
    all_to_all x1, waiting for transfers between devices, swap_strips(): lax.all_to_all(packed, 'owner', 0, 0, axis_index_groups=[owner_order], ti...  3.33 us
    dot_general x1, matrix products, shards(): jnp.einsum('bwt,tr->bwr', cotangent, activations, preferred_element_type=...  2.83 us
    dot_general x1, matrix products, shards(): jnp.dot(gradient_rows, right_matrix, precision=precision)  2.63 us
  transfers between devices with their start and end apart: 2, of which 2 were waited for; matrix products, arithmetic and copies ran while one was open for 3% of the time, Pallas kernels for 0%

profile of v2, /device:TPU:1, one launch (start us, length us, event | category | flops | bytes accessed | tf_op | source)
XLA Modules:
  0.0 117.5 jit_solution(15799331082415944709)
XLA Ops:
  0.6 0.0 copy-start
  0.6 1.6 %copy-done = bf16[32,16,2048]{2,1,0:T(8,128)(2,1)S(1)} copy-done((bf16[32,16,2048]{2,1,0:T(8,128)(2,1)S(1)}, bf16[32,16,2048]{2,1,0:T(8,128)(2,1)}, u32[]{:S(2)}) %copy-start) | copy-done | bytes 2097176
  2.2 2.8 %fusion = f32[32,16,512]{2,1,0:T(8,128)S(1)} fusion(bf16[32,16,2048]{2,1,0:T(8,128)(2,1)S(1)} %copy-done, bf16[2048,512]{1,0:T(8,128)(2,1)} %param.7), kind=kOutput, calls=%fused_computation | convolution fusion | flops 1073741824 | bytes 5242880 | tf_op jit(solution)/shard_map/bwt,tr->bwr/dot_general | solution.py:35
  5.1 0.1 copy.24
  5.1 16.5 %all_to_all.20 = f32[4,8,16,512]{3,2,0,1:T(8,128)S(1)} all-to-all(f32[4,8,16,512]{3,2,0,1:T(8,128)S(1)} %copy.24), channel_id=1, replica_groups={{0,32,64,96,128,160,192,224},{256,288,320,352,384,416,448,480},{512,544..., dimensions={1} | all-to-all | bytes 2097152 | tf_op jit(solution)/shard_map/all_to_all | solution.py:37
  21.6 0.1 reduce_sum.18
  21.7 0.7 pad_maximum_fusion
  22.4 15.2 %all-to-all-start.1 = ((f32[4,16,512]{2,1,0:T(8,128)}), f32[4,16,512]{2,1,0:T(8,128)S(1)}, u32[]{:S(2)}, u32[]{:S(2)}) async-start(f32[4,16,512]{2,1,0:T(8,128)} %pad_maximum_fusion), calls=%async_computation.1 | async-start | bytes 262144 | tf_op jit(solution)/shard_map/all_to_all | solution.py:39
  37.6 0.0 copy-start.1
  37.6 2.6 %copy.25 = f32[1,512,512]{1,2,0:T(8,128)} copy(f32[1,512,512]{2,1,0:T(8,128)} %param.10) | data formatting | bytes 2097152 | tf_op args[3]
  40.2 1.0 all-to-all-done.1
  41.2 2.6 %convolution_bitcast_fusion.1 = f32[32,16,16]{0,1,2:T(8,128)S(1)} fusion(f32[32,16,512]{2,1,0:T(8,128)} %bitcast.74, f32[16,512]{1,0:T(8,128)S(1)} %reduce_sum.19), kind=kOutput, calls=%fused_computation.3 | convolution fusion | flops 25165824 | bytes 1114112 | tf_op jit(solution)/shard_map/dot_general | solution.py:41
  43.8 0.2 copy.27
  44.0 0.1 reshape_reshape.6
  44.2 38.7 %all_to_all.21 = f32[32,2,128]{2,1,0:T(2,128)S(1)} all-to-all(f32[32,2,128]{2,1,0:T(2,128)S(1)} %bitcast.81), channel_id=1, replica_groups={{4,5,6,7,0,1,2,3,12,13,14,15,8,9,10,11,20,21,22,23,16,17,18,19,28,29,30..., dimensions={0} | all-to-all | bytes 65536 | tf_op jit(solution)/shard_map/all_to_all | solution.py:24
  82.9 0.1 reshape.51
  83.1 0.0 copy-done.1
  83.1 0.4 fusion.4
  83.4 0.0 copy-start.3
  83.4 0.6 copy-done.3
  84.1 2.2 %convolution_bitcast_fusion = f32[32,16,16]{0,1,2:T(8,128)S(1)} fusion(f32[32,16,512]{2,1,0:T(8,128)S(1)} %bitcast.73, f32[16,512]{1,0:T(8,128)S(1)} %fusion.4, f32[1,512,16]{1,2,0:T(8,128)} %param.12, f32[1,512,16]{1,2,0:T(8,128)} %param.11), kind=kOutput, calls=%fused_computation.2 | convolution fusion | flops 25255936 | bytes 1179648 | tf_op jit(solution)/shard_map/cj,ij->ci/dot_general | solution.py:46
  86.3 0.0 copy-start.2
  86.3 0.2 copy.29
  86.5 0.1 reshape_reshape.7
  86.6 0.6 pad_maximum_fusion.3
  87.3 23.4 %all-to-all-start.3 = ((f32[32,2,128]{2,1,0:T(2,128)}), f32[32,2,128]{2,1,0:T(2,128)S(1)}, u32[]{:S(2)}, u32[]{:S(2)}) async-start(f32[32,2,128]{2,1,0:T(2,128)} %bitcast.20), calls=%async_computation.3 | async-start | bytes 65536 | tf_op jit(solution)/shard_map/all_to_all | solution.py:24
  110.6 1.4 %fusion.16 = (f32[1,512,16]{1,2,0:T(8,128)}, f32[1,512,16]{1,2,0:T(8,128)}) fusion(f32[16,512]{1,0:T(8,128)} %copy-done.3, f32[1,512,16]{1,2,0:T(8,128)} %param.12, f32[1,512,16]{1,2,0:T(8,128)} %param.11), kind=kLoop, calls=%fused_computation.21 | loop fusion | flops 57344 | bytes 163840 | tf_op jit(solution)/shard_map/broadcast_in_dim | solution.py:50
  112.1 3.3 %all-to-all-done.3 = f32[32,2,128]{2,1,0:T(2,128)S(1)} async-done(((f32[32,2,128]{2,1,0:T(2,128)}), f32[32,2,128]{2,1,0:T(2,128)S(1)}, u32[]{:S(2)}, u32[]{:S(2)}) %all-to-all-start.3) | async-done | bytes 32800 | tf_op jit(solution)/shard_map/all_to_all | solution.py:24
  115.4 0.1 reshape.55
  115.6 0.0 copy-done.2
  115.6 1.3 %fusion.2 = f32[16,512]{1,0:T(8,128)S(1)} fusion(f32[16,512]{0,1:T(8,128)S(1)} %bitcast.77, f32[1,512,512]{2,1,0:T(8,128)S(1)} %copy-done.2, f32[1,16,512]{2,1,0:T(8,128)} %param.13), kind=kOutput, calls=%fused_computation.5 | convolution fusion | flops 25182208 | bytes 1146880 | tf_op jit(solution)/shard_map/ik,jk->ij/dot_general | solution.py:47
  116.9 0.0 copy-start.4
  116.9 0.6 convert_bitcast_fusion
  117.5 0.0 copy-done.4
  (9 shorter events, 0.1 us)
Async XLA Ops:
  0.6 1.6 %copy-start = (bf16[32,16,2048]{2,1,0:T(8,128)(2,1)S(1)}, bf16[32,16,2048]{2,1,0:T(8,128)(2,1)}, u32[]{:S(2)}) copy-start(bf16[32,16,2048]{2,1,0:T(8,128)(2,1)} %param.8) | copy-start | bytes 6291460
  22.4 18.8 %all-to-all-start.1 = ((f32[4,16,512]{2,1,0:T(8,128)}), f32[4,16,512]{2,1,0:T(8,128)S(1)}, u32[]{:S(2)}, u32[]{:S(2)}) async-start(f32[4,16,512]{2,1,0:T(8,128)} %pad_maximum_fusion), calls=%async_computation.1 | async-start | bytes 262144 | tf_op jit(solution)/shard_map/all_to_all | solution.py:39
  37.6 45.5 %copy-start.1 = (f32[1,512,512]{2,1,0:T(8,128)S(1)}, f32[1,512,512]{2,1,0:T(8,128)}, u32[]{:S(2)}) copy-start(f32[1,512,512]{2,1,0:T(8,128)} %param.9) | copy-start | bytes 3145732
  83.4 0.6 copy-start.3
  86.3 29.3 %copy-start.2 = (f32[1,512,512]{2,1,0:T(8,128)S(1)}, f32[1,512,512]{2,1,0:T(8,128)}, u32[]{:S(2)}) copy-start(f32[1,512,512]{2,1,0:T(8,128)} %param.10) | copy-start | bytes 3145732
  87.3 28.1 %all-to-all-start.3 = ((f32[32,2,128]{2,1,0:T(2,128)}), f32[32,2,128]{2,1,0:T(2,128)S(1)}, u32[]{:S(2)}, u32[]{:S(2)}) async-start(f32[32,2,128]{2,1,0:T(2,128)} %bitcast.20), calls=%async_computation.3 | async-start | bytes 65536 | tf_op jit(solution)/shard_map/all_to_all | solution.py:24
  116.9 0.6 copy-start.4

commit v3 on v2

v3 whole, which is shorter than its diff:
```python
import jax
import jax.numpy as jnp
from jax import lax
from jax.experimental import pallas as pl
from jax.experimental.pallas import tpu as pltpu
from jax.sharding import PartitionSpec as P

beta_one = 0.9
beta_two = 0.95
correct_one = 1.0 - 0.9**10
correct_two = 1.0 - 0.95**10
epsilon = 1e-08
learning_rate = 0.01

near_groups = [[(2 * q + p) * 4 + y for p in range(2) for y in range(4)] for q in range(4)]
quad_groups = [[(2 * q + p) * 4 + y for q in (2, 3, 0, 1)] for p in range(2) for y in range(4)]

owner_order = [(x * 4 + h) * 2 + c for x in range(4) for h in (2, 3, 0, 1) for c in range(2)]


def split(value):
    high = value.astype(jnp.bfloat16)
    return high, (value - high.astype(jnp.float32)).astype(jnp.bfloat16)


def product(left, right, contract):
    left_high, left_low = split(left)
    right_high, right_low = split(right)

    def one(x, y):
        return lax.dot_general(
            x, y, (((1,), (contract,)), ((), ())), preferred_element_type=jnp.float32
        )

    return one(left_high, right_low) + one(left_low, right_high) + one(left_high, right_high)


def pack_strips(value, tall, packed):
    tall[:, :16] = value.T
    lane = lax.broadcasted_iota(jnp.int32, (64, 128), 1) // 16
    total = jnp.zeros((64, 128), jnp.float32)
    for t in range(8):
        row = tall[pl.ds(t, 64, stride=8), :]
        if t:
            row = pltpu.roll(row, 16 * t, 1)
        total = jnp.where(lane == t, row, total)
    for tile in range(8):
        other = tile ^ 1
        packed[8 * other : 8 * other + 8, :] = total[8 * tile : 8 * tile + 8]


def unpack_strips(packed, wide):
    lane = lax.broadcasted_iota(jnp.int32, (8, 128), 1) // 16
    row = lax.broadcasted_iota(jnp.int32, (8, 128), 0)
    for half in range(2):
        for x in range(4):
            block = packed[pl.ds(16 * x + half, 8, stride=2), :]
            for step in (4, 2, 1):
                in_row = (row & step) != 0
                in_lane = (lane & step) != 0
                down = pltpu.roll(pltpu.roll(block, step, 0), 128 - 16 * step, 1)
                up = pltpu.roll(pltpu.roll(block, 8 - step, 0), 16 * step, 1)
                moved = jnp.where(in_row, down, up)
                block = jnp.where(in_row == in_lane, block, moved)
            wide[8 * half : 8 * half + 8, 128 * x : 128 * x + 128] = pltpu.roll(block, 64, 1)


def turn_kernel(far, right, packed, tall):
    rows = (far[0] + far[1]) + (far[2] + far[3])
    pack_strips(product(rows, right[...], 0), tall, packed)


def step_kernel(received, left, first, second, packed, first_out, second_out, tall, wide):
    unpack_strips(received, wide)
    rotated = product(wide[...], left[...], 0)
    first_new = beta_one * first[...] + (1.0 - beta_one) * rotated
    second_new = beta_two * second[...] + (1.0 - beta_two) * rotated * rotated
    first_out[...] = first_new
    second_out[...] = second_new
    direction = first_new / correct_one / (jnp.sqrt(second_new / correct_two) + epsilon)
    pack_strips(product(direction, left[...], 1), tall, packed)


def weight_kernel(received, right, weight, weight_out, rounded_out, wide):
    unpack_strips(received, wide)
    weight_new = weight[...] - learning_rate * product(wide[...], right[...], 1)
    weight_out[...] = weight_new
    rounded_out[...] = weight_new.astype(jnp.bfloat16)


def call(kernel, outs, scratch, flops, *args):
    moved = sum(x.size * x.dtype.itemsize for x in (*args, *outs))
    return pl.pallas_call(
        kernel,
        out_shape=outs,
        in_specs=[pl.BlockSpec(memory_space=pltpu.VMEM)] * len(args),
        out_specs=[pl.BlockSpec(memory_space=pltpu.VMEM)] * len(outs),
        scratch_shapes=[pltpu.VMEM(shape, jnp.float32) for shape in scratch],
        cost_estimate=pl.CostEstimate(flops=flops, bytes_accessed=moved, transcendentals=0),
        compiler_params=pltpu.CompilerParams(vmem_limit_bytes=16 * 2**20),
    )(*args)


def exchange(packed):
    swapped = lax.all_to_all(
        packed.reshape(32, 2, 128), "owner", 0, 0, axis_index_groups=[owner_order], tiled=True
    )
    return swapped.reshape(64, 128)


def shards(
    activations, cotangent, left_basis, right_basis, first_moment, second_moment, master_weight
):
    left_matrix = left_basis[0]
    right_matrix = right_basis[0]
    partial = jnp.einsum("bwt,tr->bwr", cotangent, activations, preferred_element_type=jnp.float32)
    partial = partial.reshape(4, 8, 16, 512)
    near = lax.all_to_all(partial, "dp", 1, 1, axis_index_groups=near_groups, tiled=True).sum(1)
    near = jnp.roll(near, 2, 0)
    far = lax.all_to_all(near, "dp", 0, 0, axis_index_groups=quad_groups, tiled=True)
    strip = jax.ShapeDtypeStruct((16, 512), jnp.float32)
    rounded = jax.ShapeDtypeStruct((16, 512), jnp.bfloat16)
    parcel = jax.ShapeDtypeStruct((64, 128), jnp.float32)
    tall, wide = (512, 128), (16, 512)
    work = 6 * 16 * 512 * 512
    (packed,) = call(turn_kernel, [parcel], [tall], work, far, right_matrix)
    packed, first_new, second_new = call(
        step_kernel,
        [parcel, strip, strip],
        [tall, wide],
        2 * work,
        exchange(packed),
        left_matrix,
        first_moment[0].T,
        second_moment[0].T,
    )
    weight_new, weight_rounded = call(
        weight_kernel, [strip, rounded], [wide], work, exchange(packed), right_matrix, master_weight[0]
    )
    return (weight_new[None], weight_rounded[None], first_new.T[None], second_new.T[None])


def solution(mesh):
    in_specs = (
        P("dp", None),
        P(None, "owner", "dp"),
        P("dp", None, None),
        P("dp", None, None),
        P("dp", None, "owner"),
        P("dp", None, "owner"),
        P("dp", "owner", None),
    )
    out_specs = (
        P("dp", "owner", None),
        P("dp", "owner", None),
        P("dp", None, "owner"),
        P("dp", None, "owner"),
    )
    return jax.shard_map(shards, mesh=mesh, in_specs=in_specs, out_specs=out_specs, check_vma=False)
```

time: 118 us -> 112 us (0.949)
  blocking collectives: 55.2 us -> 101 us
  starting transfers between devices: 38.5 us -> 0 us
  matrix products: 9.37 us -> 2.83 us
  waiting for transfers between devices: 4.31 us -> 0 us
  local copies, waits for them, and re-layouts: 5.86 us -> 1.7 us
  Pallas kernels: 0 us -> 3.85 us
  other arithmetic: 3.45 us -> 1.34 us
    all_to_all x1 -> x3, blocking collectives: 38.7 us -> 84.8 us  [the longest x2 66.1 us: exchange(): lax.all_to_all(packed.reshape(32, 2, 128), 'owner', 0, 0, axis_index_grou...]
    all_to_all x2 -> x0, starting transfers between devices: 38.5 us -> none  [the longest x1 23.4 us: swap_strips(): lax.all_to_all(packed, 'owner', 0, 0, axis_index_groups=[owner_order], ti...]
    dot_general x4 -> x0, matrix products: 6.54 us -> none  [the longest x1 2.63 us: shards(): jnp.dot(gradient_rows, right_matrix, precision=precision)]
    all_to_all x2 -> x0, waiting for transfers between devices: 4.31 us -> none  [the longest x1 3.33 us: swap_strips(): lax.all_to_all(packed, 'owner', 0, 0, axis_index_groups=[owner_order], ti...]
    pallas_call x0 -> x3, Pallas kernels: none -> 3.85 us  [call(): pl.pallas_call(kernel, out_shape=outs, in_specs=[pl.BlockSpec(memory_spac...]
    unnamed x11 -> x12, local copies, waits for them, and re-layouts: 4.85 us -> 1.61 us
    broadcast_in_dim x2 -> x0, other arithmetic: 2.04 us -> none  [the longest x1 1.43 us: shards(): second_new.T[None]]
    reduce_sum x1, other arithmetic: 0.08 us -> 1.33 us  [shards(): lax.all_to_all(partial, 'dp', 1, 1, axis_index_groups=near_groups, tiled=...]
  transfers between devices with their start and end apart: 2 -> 0, of which waited for: 2 -> 0; matrix products, arithmetic and copies ran while one was open for 3% -> 0% of each run, Pallas kernels for 0% -> 0%
where the time goes in v3:
time: 112 us
  blocking collectives  101 us (90%)
  Pallas kernels  3.85 us (3%)
  matrix products  2.83 us (3%)
  local copies, waits for them, and re-layouts  1.7 us (2%)
  other arithmetic  1.34 us (1%)
    all_to_all x2, blocking collectives, exchange(): lax.all_to_all(packed.reshape(32, 2, 128), 'owner', 0, 0, axis_index_grou...  66.1 us
    all_to_all x1, blocking collectives, shards(): lax.all_to_all(near, 'dp', 0, 0, axis_index_groups=quad_groups, tiled=True)  18.7 us
    all_to_all x1, blocking collectives, shards(): lax.all_to_all(partial, 'dp', 1, 1, axis_index_groups=near_groups, tiled=...  16.7 us
    pallas_call x3, Pallas kernels, call(): pl.pallas_call(kernel, out_shape=outs, in_specs=[pl.BlockSpec(memory_spac...  3.85 us
    dot_general x1, matrix products, shards(): jnp.einsum('bwt,tr->bwr', cotangent, activations, preferred_element_type=...  2.83 us

profile of v3, /device:TPU:1, one launch (start us, length us, event | category | flops | bytes accessed | tf_op | source)
XLA Modules:
  0.0 111.9 jit_solution(9802184581358777552)
XLA Ops:
  0.6 0.0 copy-start
  0.6 1.6 %copy-done = bf16[32,16,2048]{2,1,0:T(8,128)(2,1)S(1)} copy-done((bf16[32,16,2048]{2,1,0:T(8,128)(2,1)S(1)}, bf16[32,16,2048]{2,1,0:T(8,128)(2,1)}, u32[]{:S(2)}) %copy-start) | copy-done | bytes 2097176
  2.2 2.8 %fusion = f32[32,16,512]{2,1,0:T(8,128)S(1)} fusion(bf16[32,16,2048]{2,1,0:T(8,128)(2,1)S(1)} %copy-done, bf16[2048,512]{1,0:T(8,128)(2,1)} %param.7), kind=kOutput, calls=%fused_computation | convolution fusion | flops 1073741824 | bytes 5242880 | tf_op jit(solution)/shard_map/bwt,tr->bwr/dot_general | solution.py:116
  5.1 0.1 copy.11
  5.1 0.0 copy-start.1
  5.2 16.7 %all_to_all.20 = f32[4,8,16,512]{3,2,0,1:T(8,128)} all-to-all(f32[4,8,16,512]{3,2,0,1:T(8,128)S(1)} %copy.11), channel_id=1, replica_groups={{0,32,64,96,128,160,192,224},{256,288,320,352,384,416,448,480},{512,544..., dimensions={1} | all-to-all | bytes 2097152 | tf_op jit(solution)/shard_map/all_to_all | solution.py:118
  21.9 0.0 copy-start.3
  21.9 0.0 copy-start.4
  21.9 0.0 copy-start.5
  21.9 1.3 %reduce_sum.9 = f32[4,16,512]{2,1,0:T(8,128)S(1)} reduce(f32[4,8,16,512]{3,2,0,1:T(8,128)} %all_to_all.20, f32[]{:T(128)} %constant.0.clone.1), dimensions={1}, to_apply=%region_0.0 | reduce | flops 229376 | bytes 1179652 | tf_op jit(solution)/shard_map/reduce_sum | solution.py:118
  23.2 0.0 copy-start.2
  23.2 18.7 %all_to_all.21.far = f32[4,16,512]{2,1,0:T(8,128)S(1)} all-to-all(f32[4,16,512]{2,1,0:T(8,128)S(1)} %pad_maximum_fusion), channel_id=1, replica_groups={{512,768,0,256},{544,800,32,288},{576,832,64,320},{608,864,96,352},{640..., dimensions={0} | all-to-all | bytes 262144 | tf_op jit(solution)/shard_map/all_to_all | solution.py:120
  41.9 0.0 copy-done.1
  41.9 0.6 shard_map.102
  42.5 38.7 %all_to_all.22 = f32[32,2,128]{2,1,0:T(2,128)S(1)} all-to-all(f32[32,2,128]{2,1,0:T(2,128)S(1)} %bitcast.31), channel_id=1, replica_groups={{4,5,6,7,0,1,2,3,12,13,14,15,8,9,10,11,20,21,22,23,16,17,18,19,28,29,30..., dimensions={0} | all-to-all | bytes 65536 | tf_op jit(solution)/shard_map/all_to_all | solution.py:105
  81.3 0.0 copy-done.3
  81.3 0.0 copy-done.4
  81.3 0.0 copy-done.2
  81.3 1.9 %shard_map.103 = (f32[64,128]{1,0:T(8,128)S(1)}, f32[16,512]{1,0:T(8,128)}, f32[16,512]{1,0:T(8,128)}) custom-call(f32[64,128]{1,0:T(8,128)S(1)} %bitcast.29, f32[512,512]{1,0:T(8,128)S(1)} %bitcast.28, f32[16,512]{1,0:T(8,128)S(1)} %bitcast.32, f32[16,512]{1,0:T(8,128)S(1)} %bitcast.33), custom_call_target="tpu_custom_call" | custom-call | flops 50331648 | bytes 1245184 | tf_op jit(solution)/shard_map/pallas_call | solution.py:93
  83.2 27.3 %all_to_all.23 = f32[32,2,128]{2,1,0:T(2,128)S(1)} all-to-all(f32[32,2,128]{2,1,0:T(2,128)S(1)} %bitcast.35), channel_id=1, replica_groups={{4,5,6,7,0,1,2,3,12,13,14,15,8,9,10,11,20,21,22,23,16,17,18,19,28,29,30..., dimensions={0} | all-to-all | bytes 65536 | tf_op jit(solution)/shard_map/all_to_all | solution.py:105
  110.5 0.0 copy-done.5
  110.5 1.4 %shard_map.104 = (f32[16,512]{1,0:T(8,128)}, bf16[16,512]{1,0:T(8,128)(2,1)}) custom-call(f32[64,128]{1,0:T(8,128)S(1)} %bitcast.30, f32[512,512]{1,0:T(8,128)S(1)} %bitcast.27, f32[16,512]{1,0:T(8,128)S(1)} %bitcast.34), custom_call_target="tpu_custom_call" | custom-call | flops 25165824 | bytes 1163264 | tf_op jit(solution)/shard_map/pallas_call | solution.py:93
  (2 shorter events, 0.0 us)
Async XLA Ops:
  0.6 1.6 %copy-start = (bf16[32,16,2048]{2,1,0:T(8,128)(2,1)S(1)}, bf16[32,16,2048]{2,1,0:T(8,128)(2,1)}, u32[]{:S(2)}) copy-start(bf16[32,16,2048]{2,1,0:T(8,128)(2,1)} %param.8) | copy-start | bytes 6291460
  5.1 36.8 %copy-start.1 = (f32[1,512,512]{2,1,0:T(8,128)S(1)}, f32[1,512,512]{2,1,0:T(8,128)}, u32[]{:S(2)}) copy-start(f32[1,512,512]{2,1,0:T(8,128)} %param.10) | copy-start | bytes 3145732
  21.9 59.4 %copy-start.3 = (f32[1,512,16]{1,2,0:T(8,128)S(1)}, f32[1,512,16]{1,2,0:T(8,128)}, u32[]{:S(2)}) copy-start(f32[1,512,16]{1,2,0:T(8,128)} %param.11) | copy-start | bytes 98308
  21.9 59.4 %copy-start.4 = (f32[1,512,16]{1,2,0:T(8,128)S(1)}, f32[1,512,16]{1,2,0:T(8,128)}, u32[]{:S(2)}) copy-start(f32[1,512,16]{1,2,0:T(8,128)} %param.12) | copy-start | bytes 98308
  21.9 88.6 %copy-start.5 = (f32[1,16,512]{2,1,0:T(8,128)S(1)}, f32[1,16,512]{2,1,0:T(8,128)}, u32[]{:S(2)}) copy-start(f32[1,16,512]{2,1,0:T(8,128)} %param.13) | copy-start | bytes 98308
  23.2 58.1 %copy-start.2 = (f32[1,512,512]{2,1,0:T(8,128)S(1)}, f32[1,512,512]{2,1,0:T(8,128)}, u32[]{:S(2)}) copy-start(f32[1,512,512]{2,1,0:T(8,128)} %param.9) | copy-start | bytes 3145732

commit v4 on v3

--- a/solution.py
+++ b/solution.py
@@ -12,9 +12,8 @@
 epsilon = 1e-08
 learning_rate = 0.01
 
-near_groups = [[(2 * q + p) * 4 + y for p in range(2) for y in range(4)] for q in range(4)]
-quad_groups = [[(2 * q + p) * 4 + y for q in (2, 3, 0, 1)] for p in range(2) for y in range(4)]
-
+near_groups = [[8 * q + m for m in range(8)] for q in range(4)]
+far_groups = [[8 * q + m for q in (2, 3, 0, 1)] for m in range(8)]
 owner_order = [(x * 4 + h) * 2 + c for x in range(4) for h in (2, 3, 0, 1) for c in range(2)]
 
 
@@ -23,20 +22,28 @@
     return high, (value - high.astype(jnp.float32)).astype(jnp.bfloat16)
 
 
+def dot(left, right, contract):
+    return lax.dot_general(
+        left, right, (((1,), (contract,)), ((), ())), preferred_element_type=jnp.float32
+    )
+
+
 def product(left, right, contract):
+    high, low = split(left)
+    right_high, right_low = split(right)
+    main = dot(jnp.concatenate([high, low], 0), right_high, contract)
+    return (dot(high, right_low, contract) + main[16:]) + main[:16]
+
+
+def product_turned(left, right):
     left_high, left_low = split(left)
-    right_high, right_low = split(right)
-
-    def one(x, y):
-        return lax.dot_general(
-            x, y, (((1,), (contract,)), ((), ())), preferred_element_type=jnp.float32
-        )
-
-    return one(left_high, right_low) + one(left_low, right_high) + one(left_high, right_high)
+    high, low = split(right)
+    main = dot(left_high, jnp.concatenate([high, low], 0), 1)
+    return (dot(left_low, high, 1) + main[:, 16:]) + main[:, :16]
 
 
 def pack_strips(value, tall, packed):
-    tall[:, :16] = value.T
+    tall[:, :16] = value
     lane = lax.broadcasted_iota(jnp.int32, (64, 128), 1) // 16
     total = jnp.zeros((64, 128), jnp.float32)
     for t in range(8):
@@ -65,9 +72,72 @@
             wide[8 * half : 8 * half + 8, 128 * x : 128 * x + 128] = pltpu.roll(block, 64, 1)
 
 
+def total_of(terms):
+    while len(terms) > 1:
+        terms = [x + y for x, y in zip(terms[::2], terms[1::2])]
+    return terms[0]
+
+
+def gradient_kernel(cotangent, activations, partial, cotangent_in, activations_in, arrived):
+    near, far = partial.shape[0], partial.shape[1] // 16
+    slices, blocks, _, tokens = cotangent_in.shape
+    copies = []
+    for k in range(slices):
+        span = pl.ds(k * tokens, tokens)
+        pairs = [(activations.at[span], activations_in.at[k])]
+        for part in range(1):
+            some = pl.ds(part * blocks // 1, blocks // 1)
+            pairs.append((cotangent.at[some, :, span], cotangent_in.at[k, some]))
+        copies.append(
+            [pltpu.make_async_copy(x, y, arrived.at[k, i]) for i, (x, y) in enumerate(pairs)]
+        )
+        for copy in copies[-1]:
+            copy.start()
+    for k in range(slices):
+        for copy in copies[k]:
+            copy.wait()
+        rows = [cotangent_in[k, f * near + n] for n in range(near) for f in range(far)]
+        value = jnp.dot(
+            jnp.concatenate(rows, 0), activations_in[k], preferred_element_type=jnp.float32
+        ).reshape(partial.shape)
+        if k:
+            partial[...] += value
+        else:
+            partial[...] = value
+
+
+def gradient_partial(cotangent, activations, near):
+    blocks, rows, tokens = cotangent.shape
+    columns = activations.shape[1]
+    slices = 4
+    share = tokens // slices
+    return pl.pallas_call(
+        gradient_kernel,
+        out_shape=jax.ShapeDtypeStruct((near, blocks // near * rows, columns), jnp.float32),
+        in_specs=[pl.BlockSpec(memory_space=pl.ANY)] * 2,
+        out_specs=pl.BlockSpec(memory_space=pltpu.VMEM),
+        scratch_shapes=[
+            pltpu.VMEM((slices, blocks, rows, share), cotangent.dtype),
+            pltpu.VMEM((slices, share, columns), activations.dtype),
+            pltpu.SemaphoreType.DMA((slices, 1 + 1)),
+        ],
+        cost_estimate=pl.CostEstimate(
+            flops=2 * blocks * rows * tokens * columns, bytes_accessed=5 * 2**20, transcendentals=0
+        ),
+        compiler_params=pltpu.CompilerParams(vmem_limit_bytes=56 * 2**20),
+    )(cotangent, activations)
+
+
+def sum_kernel(near, summed):
+    far = summed.shape[0]
+    for f in range(far):
+        terms = [near[n, 16 * f : 16 * f + 16, :] for n in range(near.shape[0])]
+        summed[(f + far // 2) % far] = total_of(terms)
+
+
 def turn_kernel(far, right, packed, tall):
-    rows = (far[0] + far[1]) + (far[2] + far[3])
-    pack_strips(product(rows, right[...], 0), tall, packed)
+    rows = total_of([far[f] for f in range(far.shape[0])])
+    pack_strips(product(rows, right[...], 0).T, tall, packed)
 
 
 def step_kernel(received, left, first, second, packed, first_out, second_out, tall, wide):
@@ -78,7 +148,7 @@
     first_out[...] = first_new
     second_out[...] = second_new
     direction = first_new / correct_one / (jnp.sqrt(second_new / correct_two) + epsilon)
-    pack_strips(product(direction, left[...], 1), tall, packed)
+    pack_strips(product_turned(left[...], direction), tall, packed)
 
 
 def weight_kernel(received, right, weight, weight_out, rounded_out, wide):
@@ -113,11 +183,11 @@
 ):
     left_matrix = left_basis[0]
     right_matrix = right_basis[0]
-    partial = jnp.einsum("bwt,tr->bwr", cotangent, activations, preferred_element_type=jnp.float32)
-    partial = partial.reshape(4, 8, 16, 512)
-    near = lax.all_to_all(partial, "dp", 1, 1, axis_index_groups=near_groups, tiled=True).sum(1)
-    near = jnp.roll(near, 2, 0)
-    far = lax.all_to_all(near, "dp", 0, 0, axis_index_groups=quad_groups, tiled=True)
+    partial = gradient_partial(cotangent, activations, 8)
+    near = lax.all_to_all(partial, "dp", 0, 0, axis_index_groups=near_groups, tiled=True)
+    summed = jax.ShapeDtypeStruct((4, 16, 512), jnp.float32)
+    (near,) = call(sum_kernel, [summed], [], near.size, near)
+    far = lax.all_to_all(near, "dp", 0, 0, axis_index_groups=far_groups, tiled=True)
     strip = jax.ShapeDtypeStruct((16, 512), jnp.float32)
     rounded = jax.ShapeDtypeStruct((16, 512), jnp.bfloat16)
     parcel = jax.ShapeDtypeStruct((64, 128), jnp.float32)

time: 112 us -> 109 us (0.973)
  matrix products: 2.83 us -> 0 us
  Pallas kernels: 3.85 us -> 6.64 us
  local copies, waits for them, and re-layouts: 1.7 us -> 0.03 us
  other arithmetic: 1.34 us -> 0 us
    pallas_call x0 -> x1, Pallas kernels: none -> 3.65 us  [gradient_partial(): pl.pallas_call(gradient_kernel, out_shape=jax.ShapeDtypeStruct((near, blo...]
    dot_general x1 -> x0, matrix products: 2.83 us -> none  [shards(): jnp.einsum('bwt,tr->bwr', cotangent, activations, preferred_element_type=...]
    unnamed x12 -> x10, local copies, waits for them, and re-layouts: 1.61 us -> 0.03 us
    reduce_sum x1 -> x0, other arithmetic: 1.33 us -> none  [shards(): lax.all_to_all(partial, 'dp', 1, 1, axis_index_groups=near_groups, tiled=...]
    pallas_call x3 -> x4, Pallas kernels: 3.85 us -> 2.99 us  [call(): pl.pallas_call(kernel, out_shape=outs, in_specs=[pl.BlockSpec(memory_spac...]
where the time goes in v4:
time: 109 us
  blocking collectives  101 us (93%)
  Pallas kernels  6.64 us (6%)
    all_to_all x2, blocking collectives, exchange(): lax.all_to_all(packed.reshape(32, 2, 128), 'owner', 0, 0, axis_index_grou...  66.1 us
    all_to_all x1, blocking collectives, shards(): lax.all_to_all(near, 'dp', 0, 0, axis_index_groups=far_groups, tiled=True)  18.6 us
    all_to_all x1, blocking collectives, shards(): lax.all_to_all(partial, 'dp', 0, 0, axis_index_groups=near_groups, tiled=...  16.8 us
    pallas_call x1, Pallas kernels, gradient_partial(): pl.pallas_call(gradient_kernel, out_shape=jax.ShapeDtypeStruct((near, blo...  3.65 us
    pallas_call x4, Pallas kernels, call(): pl.pallas_call(kernel, out_shape=outs, in_specs=[pl.BlockSpec(memory_spac...  2.99 us

profile of v4, /device:TPU:1, one launch (start us, length us, event | category | flops | bytes accessed | tf_op | source)
XLA Modules:
  0.0 108.8 jit_solution(13818138523985858518)
XLA Ops:
  0.6 3.6 %shard_map.102 = f32[8,64,512]{2,1,0:T(8,128)} custom-call(bf16[32,16,2048]{2,1,0:T(8,128)(2,1)} %cotangent.1, bf16[2048,512]{1,0:T(8,128)(2,1)} %activations.1), custom_call_target="tpu_custom_call" | custom-call | flops 1073741824 | bytes 5242880 | tf_op jit(solution)/shard_map/pallas_call | solution.py:114
  4.3 0.0 copy-start
  4.3 0.0 copy-start.1
  4.3 0.0 copy-start.2
  4.3 0.0 copy-start.3
  4.3 16.8 %all_to_all.20.near = f32[8,64,512]{2,1,0:T(8,128)S(1)} all-to-all(f32[8,64,512]{2,1,0:T(8,128)} %shard_map.102), channel_id=1, replica_groups={{0,32,64,96,128,160,192,224},{256,288,320,352,384,416,448,480},{512,544..., dimensions={0} | all-to-all | bytes 2097152 | tf_op jit(solution)/shard_map/all_to_all | solution.py:187
  21.1 0.0 copy-start.4
  21.1 0.1 shard_map.103
  21.2 18.6 %all_to_all.21.far = f32[4,16,512]{2,1,0:T(8,128)S(1)} all-to-all(f32[4,16,512]{2,1,0:T(8,128)S(1)} %shard_map.103), channel_id=1, replica_groups={{512,768,0,256},{544,800,32,288},{576,832,64,320},{608,864,96,352},{640..., dimensions={0} | all-to-all | bytes 262144 | tf_op jit(solution)/shard_map/all_to_all | solution.py:190
  39.8 0.0 copy-done
  39.8 0.5 shard_map.104
  40.3 38.7 %all_to_all.22 = f32[32,2,128]{2,1,0:T(2,128)S(1)} all-to-all(f32[32,2,128]{2,1,0:T(2,128)S(1)} %bitcast.26), channel_id=1, replica_groups={{4,5,6,7,0,1,2,3,12,13,14,15,8,9,10,11,20,21,22,23,16,17,18,19,28,29,30..., dimensions={0} | all-to-all | bytes 65536 | tf_op jit(solution)/shard_map/all_to_all | solution.py:175
  79.0 0.0 copy-done.1
  79.0 0.0 copy-done.2
  79.0 0.0 copy-done.3
  79.1 1.2 %shard_map.105 = (f32[64,128]{1,0:T(8,128)S(1)}, f32[16,512]{1,0:T(8,128)}, f32[16,512]{1,0:T(8,128)}) custom-call(f32[64,128]{1,0:T(8,128)S(1)} %bitcast.24, f32[512,512]{1,0:T(8,128)S(1)} %bitcast.23, f32[16,512]{1,0:T(8,128)S(1)} %bitcast.27, f32[16,512]{1,0:T(8,128)S(1)} %bitcast.28), custom_call_target="tpu_custom_call" | custom-call | flops 50331648 | bytes 1245184 | tf_op jit(solution)/shard_map/pallas_call | solution.py:163
  80.2 27.3 %all_to_all.23 = f32[32,2,128]{2,1,0:T(2,128)S(1)} all-to-all(f32[32,2,128]{2,1,0:T(2,128)S(1)} %bitcast.30), channel_id=1, replica_groups={{4,5,6,7,0,1,2,3,12,13,14,15,8,9,10,11,20,21,22,23,16,17,18,19,28,29,30..., dimensions={0} | all-to-all | bytes 65536 | tf_op jit(solution)/shard_map/all_to_all | solution.py:175
  107.5 0.0 copy-done.4
  107.5 1.2 %shard_map.106 = (f32[16,512]{1,0:T(8,128)}, bf16[16,512]{1,0:T(8,128)(2,1)}) custom-call(f32[64,128]{1,0:T(8,128)S(1)} %bitcast.25, f32[512,512]{1,0:T(8,128)S(1)} %bitcast.22, f32[16,512]{1,0:T(8,128)S(1)} %bitcast.29), custom_call_target="tpu_custom_call" | custom-call | flops 25165824 | bytes 1163264 | tf_op jit(solution)/shard_map/pallas_call | solution.py:163
Async XLA Ops:
  4.3 35.5 %copy-start = (f32[1,512,512]{2,1,0:T(8,128)S(1)}, f32[1,512,512]{2,1,0:T(8,128)}, u32[]{:S(2)}) copy-start(f32[1,512,512]{2,1,0:T(8,128)} %param.10) | copy-start | bytes 3145732
  4.3 74.7 %copy-start.1 = (f32[1,512,512]{2,1,0:T(8,128)S(1)}, f32[1,512,512]{2,1,0:T(8,128)}, u32[]{:S(2)}) copy-start(f32[1,512,512]{2,1,0:T(8,128)} %param.9) | copy-start | bytes 3145732
  4.3 74.7 %copy-start.2 = (f32[1,512,16]{1,2,0:T(8,128)S(1)}, f32[1,512,16]{1,2,0:T(8,128)}, u32[]{:S(2)}) copy-start(f32[1,512,16]{1,2,0:T(8,128)} %param.11) | copy-start | bytes 98308
  4.3 74.7 %copy-start.3 = (f32[1,512,16]{1,2,0:T(8,128)S(1)}, f32[1,512,16]{1,2,0:T(8,128)}, u32[]{:S(2)}) copy-start(f32[1,512,16]{1,2,0:T(8,128)} %param.12) | copy-start | bytes 98308
  21.1 86.4 %copy-start.4 = (f32[1,16,512]{2,1,0:T(8,128)S(1)}, f32[1,16,512]{2,1,0:T(8,128)}, u32[]{:S(2)}) copy-start(f32[1,16,512]{2,1,0:T(8,128)} %param.13) | copy-start | bytes 98308

commit v5 on v4

--- a/solution.py
+++ b/solution.py
@@ -14,7 +14,8 @@
 
 near_groups = [[8 * q + m for m in range(8)] for q in range(4)]
 far_groups = [[8 * q + m for q in (2, 3, 0, 1)] for m in range(8)]
-owner_order = [(x * 4 + h) * 2 + c for x in range(4) for h in (2, 3, 0, 1) for c in range(2)]
+layer_order = (2, 0, 1, 3)
+owner_order = [(x * 4 + h) * 2 + c for h in layer_order for x in range(4) for c in range(2)]
 
 
 def split(value):
@@ -51,17 +52,22 @@
         if t:
             row = pltpu.roll(row, 16 * t, 1)
         total = jnp.where(lane == t, row, total)
-    for tile in range(8):
-        other = tile ^ 1
-        packed[8 * other : 8 * other + 8, :] = total[8 * tile : 8 * tile + 8]
-
-
-def unpack_strips(packed, wide):
+    for spot, layer in enumerate(layer_order):
+        for x in range(4):
+            here, there = 16 * spot + 4 * x, 16 * x + 4 * layer
+            packed[here : here + 4, :] = total[there : there + 4]
+
+
+def unpack_strips(packed, ordered, wide):
     lane = lax.broadcasted_iota(jnp.int32, (8, 128), 1) // 16
     row = lax.broadcasted_iota(jnp.int32, (8, 128), 0)
+    for spot, layer in enumerate(layer_order):
+        for x in range(4):
+            here, there = 16 * spot + 4 * x, 16 * x + 4 * layer
+            ordered[there : there + 4, :] = packed[here : here + 4, :]
     for half in range(2):
         for x in range(4):
-            block = packed[pl.ds(16 * x + half, 8, stride=2), :]
+            block = ordered[pl.ds(16 * x + half, 8, stride=2), :]
             for step in (4, 2, 1):
                 in_row = (row & step) != 0
                 in_lane = (lane & step) != 0
@@ -69,7 +75,7 @@
                 up = pltpu.roll(pltpu.roll(block, 8 - step, 0), 16 * step, 1)
                 moved = jnp.where(in_row, down, up)
                 block = jnp.where(in_row == in_lane, block, moved)
-            wide[8 * half : 8 * half + 8, 128 * x : 128 * x + 128] = pltpu.roll(block, 64, 1)
+            wide[8 * half : 8 * half + 8, 128 * x : 128 * x + 128] = block
 
 
 def total_of(terms):
@@ -140,8 +146,8 @@
     pack_strips(product(rows, right[...], 0).T, tall, packed)
 
 
-def step_kernel(received, left, first, second, packed, first_out, second_out, tall, wide):
-    unpack_strips(received, wide)
+def step_kernel(received, left, first, second, packed, first_out, second_out, tall, ordered, wide):
+    unpack_strips(received, ordered, wide)
     rotated = product(wide[...], left[...], 0)
     first_new = beta_one * first[...] + (1.0 - beta_one) * rotated
     second_new = beta_two * second[...] + (1.0 - beta_two) * rotated * rotated
@@ -151,8 +157,8 @@
     pack_strips(product_turned(left[...], direction), tall, packed)
 
 
-def weight_kernel(received, right, weight, weight_out, rounded_out, wide):
-    unpack_strips(received, wide)
+def weight_kernel(received, right, weight, weight_out, rounded_out, ordered, wide):
+    unpack_strips(received, ordered, wide)
     weight_new = weight[...] - learning_rate * product(wide[...], right[...], 1)
     weight_out[...] = weight_new
     rounded_out[...] = weight_new.astype(jnp.bfloat16)
@@ -197,7 +203,7 @@
     packed, first_new, second_new = call(
         step_kernel,
         [parcel, strip, strip],
-        [tall, wide],
+        [tall, (64, 128), wide],
         2 * work,
         exchange(packed),
         left_matrix,
@@ -205,7 +211,7 @@
         second_moment[0].T,
     )
     weight_new, weight_rounded = call(
-        weight_kernel, [strip, rounded], [wide], work, exchange(packed), right_matrix, master_weight[0]
+        weight_kernel, [strip, rounded], [(64, 128), wide], work, exchange(packed), right_matrix, master_weight[0]
     )
     return (weight_new[None], weight_rounded[None], first_new.T[None], second_new.T[None])
 

time: 109 us -> 109 us (level)
  no operation moved by 1% of the time
where the time goes in v5:
time: 109 us
  blocking collectives  101 us (93%)
  Pallas kernels  6.52 us (6%)
    all_to_all x2, blocking collectives, exchange(): lax.all_to_all(packed.reshape(32, 2, 128), 'owner', 0, 0, axis_index_grou...  66.1 us
    all_to_all x1, blocking collectives, shards(): lax.all_to_all(near, 'dp', 0, 0, axis_index_groups=far_groups, tiled=True)  18.6 us
    all_to_all x1, blocking collectives, shards(): lax.all_to_all(partial, 'dp', 0, 0, axis_index_groups=near_groups, tiled=...  16.8 us
    pallas_call x1, Pallas kernels, gradient_partial(): pl.pallas_call(gradient_kernel, out_shape=jax.ShapeDtypeStruct((near, blo...  3.65 us
    pallas_call x4, Pallas kernels, call(): pl.pallas_call(kernel, out_shape=outs, in_specs=[pl.BlockSpec(memory_spac...  2.87 us

profile of v5, /device:TPU:1, one launch (start us, length us, event | category | flops | bytes accessed | tf_op | source)
XLA Modules:
  0.0 108.7 jit_solution(3881777201804996524)
XLA Ops:
  0.6 3.6 %shard_map.102 = f32[8,64,512]{2,1,0:T(8,128)} custom-call(bf16[32,16,2048]{2,1,0:T(8,128)(2,1)} %cotangent.1, bf16[2048,512]{1,0:T(8,128)(2,1)} %activations.1), custom_call_target="tpu_custom_call" | custom-call | flops 1073741824 | bytes 5242880 | tf_op jit(solution)/shard_map/pallas_call | solution.py:120
  4.3 0.0 copy-start
  4.3 0.0 copy-start.1
  4.3 0.0 copy-start.2
  4.3 0.0 copy-start.3
  4.3 16.8 %all_to_all.20.near = f32[8,64,512]{2,1,0:T(8,128)S(1)} all-to-all(f32[8,64,512]{2,1,0:T(8,128)} %shard_map.102), channel_id=1, replica_groups={{0,32,64,96,128,160,192,224},{256,288,320,352,384,416,448,480},{512,544..., dimensions={0} | all-to-all | bytes 2097152 | tf_op jit(solution)/shard_map/all_to_all | solution.py:193
  21.1 0.0 copy-start.4
  21.1 0.1 shard_map.103
  21.2 18.6 %all_to_all.21.far = f32[4,16,512]{2,1,0:T(8,128)S(1)} all-to-all(f32[4,16,512]{2,1,0:T(8,128)S(1)} %shard_map.103), channel_id=1, replica_groups={{512,768,0,256},{544,800,32,288},{576,832,64,320},{608,864,96,352},{640..., dimensions={0} | all-to-all | bytes 262144 | tf_op jit(solution)/shard_map/all_to_all | solution.py:196
  39.8 0.0 copy-done
  39.8 0.5 shard_map.104
  40.3 38.9 %all_to_all.22 = f32[32,2,128]{2,1,0:T(2,128)S(1)} all-to-all(f32[32,2,128]{2,1,0:T(2,128)S(1)} %bitcast.26), channel_id=1, replica_groups={{4,5,12,13,20,21,28,29,0,1,8,9,16,17,24,25,2,3,10,11,18,19,26,27,6,7,14..., dimensions={0} | all-to-all | bytes 65536 | tf_op jit(solution)/shard_map/all_to_all | solution.py:181
  79.2 0.0 copy-done.1
  79.2 0.0 copy-done.2
  79.2 0.0 copy-done.3
  79.2 1.1 %shard_map.105 = (f32[64,128]{1,0:T(8,128)S(1)}, f32[16,512]{1,0:T(8,128)}, f32[16,512]{1,0:T(8,128)}) custom-call(f32[64,128]{1,0:T(8,128)S(1)} %bitcast.24, f32[512,512]{1,0:T(8,128)S(1)} %bitcast.23, f32[16,512]{1,0:T(8,128)S(1)} %bitcast.27, f32[16,512]{1,0:T(8,128)S(1)} %bitcast.28), custom_call_target="tpu_custom_call" | custom-call | flops 50331648 | bytes 1245184 | tf_op jit(solution)/shard_map/pallas_call | solution.py:169
  80.3 27.2 %all_to_all.23 = f32[32,2,128]{2,1,0:T(2,128)S(1)} all-to-all(f32[32,2,128]{2,1,0:T(2,128)S(1)} %bitcast.30), channel_id=1, replica_groups={{4,5,12,13,20,21,28,29,0,1,8,9,16,17,24,25,2,3,10,11,18,19,26,27,6,7,14..., dimensions={0} | all-to-all | bytes 65536 | tf_op jit(solution)/shard_map/all_to_all | solution.py:181
  107.5 0.0 copy-done.4
  107.5 1.2 %shard_map.106 = (f32[16,512]{1,0:T(8,128)}, bf16[16,512]{1,0:T(8,128)(2,1)}) custom-call(f32[64,128]{1,0:T(8,128)S(1)} %bitcast.25, f32[512,512]{1,0:T(8,128)S(1)} %bitcast.22, f32[16,512]{1,0:T(8,128)S(1)} %bitcast.29), custom_call_target="tpu_custom_call" | custom-call | flops 25165824 | bytes 1163264 | tf_op jit(solution)/shard_map/pallas_call | solution.py:169
Async XLA Ops:
  4.3 35.5 %copy-start = (f32[1,512,512]{2,1,0:T(8,128)S(1)}, f32[1,512,512]{2,1,0:T(8,128)}, u32[]{:S(2)}) copy-start(f32[1,512,512]{2,1,0:T(8,128)} %param.10) | copy-start | bytes 3145732
  4.3 74.9 %copy-start.1 = (f32[1,512,512]{2,1,0:T(8,128)S(1)}, f32[1,512,512]{2,1,0:T(8,128)}, u32[]{:S(2)}) copy-start(f32[1,512,512]{2,1,0:T(8,128)} %param.9) | copy-start | bytes 3145732
  4.3 74.8 %copy-start.2 = (f32[1,512,16]{1,2,0:T(8,128)S(1)}, f32[1,512,16]{1,2,0:T(8,128)}, u32[]{:S(2)}) copy-start(f32[1,512,16]{1,2,0:T(8,128)} %param.11) | copy-start | bytes 98308
  4.3 74.8 %copy-start.3 = (f32[1,512,16]{1,2,0:T(8,128)S(1)}, f32[1,512,16]{1,2,0:T(8,128)}, u32[]{:S(2)}) copy-start(f32[1,512,16]{1,2,0:T(8,128)} %param.12) | copy-start | bytes 98308
  21.1 86.4 %copy-start.4 = (f32[1,16,512]{2,1,0:T(8,128)S(1)}, f32[1,16,512]{2,1,0:T(8,128)}, u32[]{:S(2)}) copy-start(f32[1,16,512]{2,1,0:T(8,128)} %param.13) | copy-start | bytes 98308
